TPU v7x, 128 devices: a whole 4x4x4 slice. The times are simulated.
128 devices in a mesh: seq: 16 (over x, y), enc: 8 (over z, core).
Axes of the slice: x: 4, y: 4, z: 4, core: 2. Of those that a mesh axis runs over, the one named last changes fastest.
Arguments:
- queries: bfloat16 [8192, 4096], P('seq', 'enc'), may hold values from -288 to 288
- out_grad: bfloat16 [8192, 4096], P('seq', 'enc'), may hold values from -48 to 48
- enc_table: bfloat16 [1024, 896, 128], P('seq', 'enc'), may hold values from -6 to 6
- key_weight: bfloat16 [896, 4096], P(None, 'enc'), may hold values from -0.1875 to 0.1875
- value_weight: bfloat16 [896, 4096], P(None, 'enc'), may hold values from -0.1875 to 0.1875
- neighbour_owner: int32 [128, 2], P('seq'), may hold values from 0 to 15, all different within a row; in each aligned block of 8 rows (0 to 7, 8 to 15, ...) at most 2 rows name the same one
- neighbour_row: int32 [128, 2], P('seq'), may hold values from 0 to 63
Outputs:
- d_query: bfloat16 [8192, 4096], P('seq', 'enc')
- d_table: float32 [1024, 896, 128], P('seq', 'enc')
Inputs may be any that keep to these rules, and one draw needn't show every extreme that they name: `neighbour_owner`: the 2 neighbours of a span have different owners. Among the 8 rows of one index of seq, no owner is named more than 2 times, a bound that some block reaches.
All inputs are finite; a program needn't handle non-finite values.
Results may differ from a plain program's by a relative error of at most 0.025.
The roundings to bfloat16 on the way count: a program that leaves them out, or rounds other values in their place, can miss the bound.
Values may be sent and summed in bfloat16 or wider, within the bound.
A program may use at most 128 MiB of HBM per device.

v0:
```python
import math

import jax
import jax.numpy as jnp
from jax import lax
from jax.sharding import PartitionSpec as P

M = 64
KN = 2
R = 128
DE = 896
DH = 128
SEQ_LEN = 2048


def passed_along(x, axis, by):
    count = lax.axis_size(axis)
    pairs = [(i, i + by) for i in range(count) if 0 <= i + by < count]
    return lax.ppermute(x, axis, pairs)


def attend_block(shifted, gradient, keys, values, score_scale):
    scores = (
        jnp.einsum("cmhd,ckhd->chmk", shifted, keys, preferred_element_type=jnp.float32)
        * score_scale
    )
    weights = jax.nn.softmax(scores, axis=-1)
    rounded = weights.astype(jnp.bfloat16)
    attended = jnp.einsum("chmk,ckhd->cmhd", rounded, values, preferred_element_type=jnp.float32)
    row_delta = jnp.transpose(jnp.sum(gradient.astype(jnp.float32) * attended, axis=-1), (0, 2, 1))
    value_grad = jnp.einsum(
        "chmk,cmhd->ckhd", rounded, gradient, preferred_element_type=jnp.float32
    ).astype(jnp.bfloat16)
    product = jnp.einsum("cmhd,ckhd->chmk", gradient, values, preferred_element_type=jnp.float32)
    score_grad = (weights * (product - row_delta[..., None])).astype(jnp.bfloat16)
    query_grad = (
        jnp.einsum("chmk,ckhd->cmhd", score_grad, keys, preferred_element_type=jnp.float32)
        * score_scale
    )
    key_grad = (
        jnp.einsum("chmk,cmhd->ckhd", score_grad, shifted, preferred_element_type=jnp.float32)
        * score_scale
    ).astype(jnp.bfloat16)
    return (query_grad, key_grad, value_grad)


def local(queries, out_grad, enc_table, key_weight, value_weight, neighbour_owner, neighbour_row):
    tok_rows, head_columns = queries.shape
    head_count = head_columns // DH
    span_count = tok_rows // M
    use_count = span_count * KN
    seq_count = lax.axis_size("seq")
    enc_count = lax.axis_size("enc")
    slot_cap = max(2, 3 * ((use_count + seq_count - 1) // seq_count) // 2)
    slot_total = seq_count * slot_cap
    block_count = enc_table.shape[0]
    column_width = enc_table.shape[1]
    score_scale = 1.0 / math.sqrt(DH)
    zero_value = jnp.zeros((), jnp.bfloat16)
    leading = jnp.stack([queries[:M], out_grad[:M]])
    following = passed_along(leading, "seq", -1)
    rows_global = lax.axis_index("seq") * tok_rows + lax.iota(jnp.int32, tok_rows)
    in_sequence = rows_global % SEQ_LEN <= SEQ_LEN - M
    shifted = jnp.where(
        in_sequence[:, None],
        jnp.concatenate([queries[M - 1 :], following[0, : M - 1]], 0),
        zero_value,
    )
    shifted_grad = jnp.where(
        in_sequence[:, None],
        jnp.concatenate([out_grad[M - 1 :], following[1, : M - 1]], 0),
        zero_value,
    )
    owners = neighbour_owner.reshape(use_count)
    row_ids = neighbour_row.reshape(use_count)
    positions = lax.iota(jnp.int32, use_count)
    earlier = (owners[:, None] == owners[None, :]) & (positions[None, :] < positions[:, None])
    ranking = jnp.sum(earlier.astype(jnp.int32), axis=1)
    slot_index = owners * slot_cap + ranking
    request = jnp.full((slot_total,), -1, jnp.int32).at[slot_index].set(row_ids)
    requested = lax.all_to_all(request, "seq", split_axis=0, concat_axis=0, tiled=True)
    present = requested >= 0
    picked = jnp.where(present[:, None, None], enc_table[jnp.maximum(requested, 0)], zero_value)
    joint_weight = jnp.concatenate([key_weight, value_weight], 1)
    copies = jnp.broadcast_to(picked[:, None, :, :], (slot_total, enc_count, column_width, R))
    arrived = lax.all_to_all(
        lax.all_to_all(copies, "seq", split_axis=0, concat_axis=0, tiled=True),
        "enc",
        split_axis=1,
        concat_axis=1,
        tiled=True,
    )
    gathered = arrived.reshape(slot_total, enc_count * column_width, R)[slot_index]
    projected = jnp.einsum(
        "udr,dc->urc", gathered, joint_weight, preferred_element_type=jnp.float32
    ).reshape(use_count * R, 2 * head_columns)
    key_value = projected.astype(jnp.bfloat16)
    keys = key_value[:, :head_columns].reshape(span_count, KN * R, head_count, DH)
    values = key_value[:, head_columns:].reshape(span_count, KN * R, head_count, DH)
    query_grad, key_grad, value_grad = attend_block(
        shifted.reshape(span_count, M, head_count, DH),
        shifted_grad.reshape(span_count, M, head_count, DH),
        keys,
        values,
        score_scale,
    )
    dq_rounded = query_grad.reshape(tok_rows, head_columns).astype(jnp.bfloat16)
    previous = passed_along(dq_rounded[tok_rows - M :], "seq", 1)
    d_query = jnp.concatenate([previous[1:], dq_rounded[: tok_rows - M + 1]], 0)
    both_grads = jnp.concatenate(
        [
            key_grad.reshape(use_count, R, head_columns),
            value_grad.reshape(use_count, R, head_columns),
        ],
        2,
    )
    partial_value = jnp.einsum(
        "urc,dc->udr", both_grads, joint_weight, preferred_element_type=jnp.float32
    )
    placed = jnp.zeros((slot_total, DE, R), jnp.float32).at[slot_index].set(partial_value)
    returned = lax.all_to_all(
        lax.all_to_all(
            placed.reshape(slot_total, enc_count, column_width, R),
            "seq",
            split_axis=0,
            concat_axis=0,
            tiled=True,
        ),
        "enc",
        split_axis=1,
        concat_axis=1,
        tiled=True,
    )
    summed = jnp.sum(returned, axis=1)
    selector = (lax.iota(jnp.int32, block_count)[:, None] == requested[None, :]).astype(jnp.float32)
    d_table = jnp.dot(
        selector,
        summed.reshape(slot_total, column_width * R),
        precision=lax.Precision.HIGHEST,
        preferred_element_type=jnp.float32,
    )
    return (d_query, d_table.reshape(block_count, column_width, R))


def solution(mesh):
    in_specs = (
        P("seq", "enc"),
        P("seq", "enc"),
        P("seq", "enc", None),
        P(None, "enc"),
        P(None, "enc"),
        P("seq", None),
        P("seq", None),
    )
    out_specs = (P("seq", "enc"), P("seq", "enc", None))
    return jax.shard_map(local, mesh=mesh, in_specs=in_specs, out_specs=out_specs, check_vma=False)
```

profile of v0, /device:TPU:32, one launch (start us, length us, event | category | flops | bytes accessed | tf_op | source)
XLA Modules:
  0.0 666.8 jit_solution(18294792935671020829)
XLA Ops:
  0.6 0.0 copy-start
  0.6 0.8 broadcast_multiply_fusion
  1.5 0.8 copy.81
  2.2 0.1 copy.80
  2.3 0.1 mul.43
  2.4 0.8 copy.82
  3.1 0.1 reshape.151
  3.2 0.1 eq.30
  3.3 0.2 convert_reduce_fusion
  3.5 0.6 scatter_custom_fusion
  4.1 0.1 all_to_all.20
  4.2 14.4 %all_to_all.32 = s32[16,2,1]{1,2,0:T(1,128)S(1)} all-to-all(s32[16,2,1]{1,2,0:T(1,128)S(1)} %bitcast.77), channel_id=1, replica_groups=mesh['seq'=16,'enc'=8] {'seq'}, dimensions={0} | all-to-all | bytes 256 | tf_op jit(solution)/shard_map/all_to_all | solution.py:81
  18.6 0.5 broadcast.137
  19.1 0.7 fusion.73
  19.8 0.1 all_to_all.22
  19.9 0.1 reshape.133
  20.0 0.7 gather_fusion
  20.8 0.1 broadcast_select_fusion
  20.9 0.9 broadcast_in_dim.57
  21.8 86.5 %all_to_all.33 = bf16[32,8,112,128]{3,2,1,0:T(8,128)(2,1)S(1)} all-to-all(bf16[32,8,112,128]{3,2,1,0:T(8,128)(2,1)S(1)} %broadcast_in_dim.57), channel_id=1, replica_groups=mesh['seq'=16,'enc'=8] {'seq'}, dimensions={0} | all-to-all | bytes 14680064 | tf_op jit(solution)/shard_map/all_to_all | solution.py:87
  108.3 4.4 copy.84
  112.7 5.5 all-to-all-start.2
  118.2 0.0 copy-done.4
  118.3 1.3 collective-permute-start
  119.6 0.1 slice.37
  119.7 0.1 slice.41
  119.9 5.9 collective-permute-done
  125.8 0.1 concatenate.21
  126.0 0.1 concatenate.23
  126.1 74.2 %all-to-all-done.2 = bf16[32,8,112,128]{3,2,0,1:T(8,128)(2,1)} async-done(((bf16[32,8,112,128]{3,2,0,1:T(8,128)(2,1)}), bf16[32,8,112,128]{3,2,0,1:T(8,128)(2,1)}, u32[]{:S(2)}, u32[]{:S(2)}) %all-to-all-start.2) | async-done | bytes 7340064 | tf_op jit(solution)/shard_map/all_to_all | solution.py:86
  200.3 8.2 %copy.85 = bf16[32,8,112,128]{3,2,1,0:T(8,128)(2,1)} copy(bf16[32,8,112,128]{3,2,0,1:T(8,128)(2,1)} %all-to-all-done.2) | data formatting | bytes 14680064 | tf_op jit(solution)/shard_map/all_to_all | solution.py:86
  208.4 6.0 gather_fusion.1
  214.5 0.0 copy-done.5
  214.5 6.8 %convolution_convert_fusion = bf16[16,128,1024]{2,1,0:T(8,128)(2,1)S(1)} fusion(bf16[16,896,128]{2,1,0:T(8,128)(2,1)} %gather_fusion.1, bf16[896,512]{1,0:T(8,128)(2,1)S(1)} %copy-done.5, bf16[896,512]{1,0:T(8,128)(2,1)} %param.10), kind=kOutput, calls=%fused_computation.11 | convolution fusion | flops 3763863552 | bytes 9699328 | tf_op jit(solution)/shard_map/udr,dc->urc/dot_general | solution.py:94
  221.3 2.3 fusion.74
  223.6 4.0 reshape.174
  227.6 4.0 reshape.175
  231.6 2.5 fusion.13
  234.1 2.0 fusion.75
  236.1 7.1 %convert_bitcast_fusion = bf16[8,256,4,128]{1,3,2,0:T(8,128)(2,1)} fusion(bf16[8,64,4,128]{3,2,1,0:T(4,128)(2,1)S(1)} %concatenate.23, pred[8,64]{1,0:T(8,128)(4,1)S(1)} %fusion.52, f32[8,4,64]{2,1,0:T(4,128)S(1)} %get-tuple-element.18, f32[8,4,64,256]{3,2,1,0:T(8,128)} %copy-done.2), kind=kOutput, calls=%fused_computation.12 | convolution fusion | flops 137627904 | bytes 4727296 | tf_op jit(solution)/shard_map/chmk,cmhd->ckhd/dot_general | solution.py:31
  243.2 6.2 fusion.35
  249.4 4.2 copy.106
  253.7 4.1 reshape.167
  257.8 3.7 multiply_convert_fusion.1
  261.5 2.5 fusion.20
  264.0 4.3 copy.105
  268.3 4.2 reshape.166
  272.5 7.9 %fusion.5 = f32[16,896,128]{2,1,0:T(8,128)} fusion(bf16[16,128,512]{2,1,0:T(8,128)(2,1)} %reshape.167, bf16[16,128,512]{2,1,0:T(8,128)(2,1)} %reshape.166, bf16[896,512]{1,0:T(8,128)(2,1)S(1)} %copy-done.6, bf16[896,512]{1,0:T(8,128)(2,1)} %param.10), kind=kOutput, calls=%fused_computation.10 | convolution fusion | flops 3770155008 | bytes 13369344 | tf_op jit(solution)/shard_map/urc,dc->udr/dot_general | solution.py:117
  280.4 6.9 %broadcast_in_dim.60 = f32[32,896,128]{2,1,0:T(8,128)} broadcast(f32[]{:T(128)} %constant.49.clone.1), dimensions={} | broadcast | bytes 14680068 | tf_op jit(solution)/shard_map/broadcast_in_dim | solution.py:120
  287.3 14.2 %scatter_fusion = f32[32,896,128]{2,1,0:T(8,128)} fusion(f32[32,896,128]{2,1,0:T(8,128)} %broadcast_in_dim.60, s32[16]{0:T(128)S(1)} %fusion.53, f32[16,896,128]{2,1,0:T(8,128)} %fusion.5), kind=kCustom, calls=%fused_computation.3 | custom fusion | bytes 22020160 | tf_op jit(solution)/shard_map/scatter | solution.py:120
  301.5 168.8 %all_to_all.34 = f32[32,8,112,128]{3,2,1,0:T(8,128)} all-to-all(f32[32,8,112,128]{3,2,1,0:T(8,128)} %bitcast.69), channel_id=1, replica_groups=mesh['seq'=16,'enc'=8] {'seq'}, dimensions={0} | all-to-all | bytes 29360128 | tf_op jit(solution)/shard_map/all_to_all | solution.py:122
  470.3 11.8 %copy.101 = f32[32,8,112,128]{3,2,0,1:T(8,128)} copy(f32[32,8,112,128]{3,2,1,0:T(8,128)} %all_to_all.34) | data formatting | bytes 29360128 | tf_op jit(solution)/shard_map/all_to_all | solution.py:122
  482.1 8.8 %all-to-all-start.4 = ((f32[32,8,112,128]{3,2,0,1:T(8,128)}), f32[32,8,112,128]{3,2,0,1:T(8,128)}, u32[]{:S(2)}, u32[]{:S(2)}) async-start(f32[32,8,112,128]{3,2,0,1:T(8,128)} %copy.101), calls=%async_computation.4 | async-start | bytes 29360128 | tf_op jit(solution)/shard_map/all_to_all | solution.py:121
  490.8 2.0 fusion.38
  492.9 0.1 copy.95
  493.0 2.2 collective-permute-start.1
  495.1 0.4 copy.96
  495.6 0.1 copy.158
  495.7 1.3 collective-permute-done.1
  497.1 0.9 pad_maximum_fusion.2
  498.0 153.6 %all-to-all-done.4 = f32[32,8,112,128]{3,2,0,1:T(8,128)} async-done(((f32[32,8,112,128]{3,2,0,1:T(8,128)}), f32[32,8,112,128]{3,2,0,1:T(8,128)}, u32[]{:S(2)}, u32[]{:S(2)}) %all-to-all-start.4) | async-done | bytes 14680096 | tf_op jit(solution)/shard_map/all_to_all | solution.py:121
  651.5 7.5 %reduce_sum.42 = f32[32,112,128]{2,1,0:T(8,128)} reduce(f32[32,8,112,128]{3,2,0,1:T(8,128)} %all-to-all-done.4, f32[]{:T(128)} %constant.49.clone.1), dimensions={1}, to_apply=%region_6.7 | reduce | flops 3211264 | bytes 16515076 | tf_op jit(solution)/shard_map/reduce_sum | solution.py:134
  659.0 3.8 fusion.17
  662.9 4.0 copy.103
  (25 shorter events, 0.3 us)
Async XLA Ops:
  0.6 19.4 %copy-start = (bf16[64,112,128]{2,1,0:T(8,128)(2,1)S(1)}, bf16[64,112,128]{2,1,0:T(8,128)(2,1)}, u32[]{:S(2)}) copy-start(bf16[64,112,128]{2,1,0:T(8,128)(2,1)} %param.9) | copy-start | bytes 5505028
  112.7 5.6 copy-start.3
  112.7 5.6 copy-start.4
  112.7 87.6 %all-to-all-start.2 = ((bf16[32,8,112,128]{3,2,0,1:T(8,128)(2,1)}), bf16[32,8,112,128]{3,2,0,1:T(8,128)(2,1)}, u32[]{:S(2)}, u32[]{:S(2)}) async-start(bf16[32,8,112,128]{3,2,0,1:T(8,128)(2,1)} %copy.84), calls=%async_computation.2 | async-start | bytes 14680064 | tf_op jit(solution)/shard_map/all_to_all | solution.py:86
  118.3 7.4 %collective-permute-start = (bf16[2,64,512]{2,1,0:T(8,128)(2,1)S(1)}, bf16[2,64,512]{2,1,0:T(8,128)(2,1)S(1)}, u32[]{:S(2)}, u32[]{:S(2)}) collective-permute-start(bf16[2,64,512]{2,1,0:T(8,128)(2,1)S(1)} %pad_maximum_fusion.3), channel_id=1, source_target_pairs={{8,0},{16,8},{24,16},{32,24},{40,32},{48,40},{56,48},{64,56},{72,6... | collective-permute-start | bytes 393224 | tf_op jit(solution)/shard_map/ppermute | solution.py:19
  208.4 6.0 copy-start.5
  234.0 2.0 copy-start.2
  268.3 4.2 copy-start.6
  482.1 169.5 %all-to-all-start.4 = ((f32[32,8,112,128]{3,2,0,1:T(8,128)}), f32[32,8,112,128]{3,2,0,1:T(8,128)}, u32[]{:S(2)}, u32[]{:S(2)}) async-start(f32[32,8,112,128]{3,2,0,1:T(8,128)} %copy.101), calls=%async_computation.4 | async-start | bytes 29360128 | tf_op jit(solution)/shard_map/all_to_all | solution.py:121
  493.0 4.0 collective-permute-start.1
  659.0 7.8 %copy-start.1 = (bf16[64,112,128]{2,1,0:T(8,128)(2,1)S(1)}, bf16[64,112,128]{2,1,0:T(8,128)(2,1)}, u32[]{:S(2)}) copy-start(bf16[64,112,128]{2,1,0:T(8,128)(2,1)} %param.9) | copy-start | bytes 5505028
where the time goes:
time: 670 us; the launch traced here: 667 us
  blocking collectives  270 us (40%)
  waiting for transfers between devices  235 us (35%)
  local copies, waits for them, and re-layouts  88.6 us (13%)
  matrix products  42.6 us (6%)
  starting transfers between devices  17.8 us (3%)
  other arithmetic  12.4 us (2%)
    all_to_all x1, blocking collectives, local(): lax.all_to_all(placed.reshape(slot_total, enc_count, column_width, R), 's...  169 us
    all_to_all x1, waiting for transfers between devices, local(): lax.all_to_all(lax.all_to_all(placed.reshape(slot_total, enc_count, colum...  154 us
    all_to_all x1, blocking collectives, local(): lax.all_to_all(copies, 'seq', split_axis=0, concat_axis=0, tiled=True)  86.5 us
    all_to_all x1, waiting for transfers between devices, local(): lax.all_to_all(lax.all_to_all(copies, 'seq', split_axis=0, concat_axis=0,...  74.2 us
    all_to_all x1, blocking collectives, local(): lax.all_to_all(request, 'seq', split_axis=0, concat_axis=0, tiled=True)  14.4 us
    scatter x1, local copies, waits for them, and re-layouts, local(): jnp.zeros((slot_total, DE, R), jnp.float32).at[slot_index]  14.2 us
  transfers between devices with their start and end apart: 4, of which 4 were waited for; matrix products, arithmetic and copies ran while one was open for 1% of the time, Pallas kernels for 0%

commit v1 on v0

v1 whole, which is shorter than its diff:
```python
import functools
import math

import jax
import jax.numpy as jnp
from jax import lax
from jax.experimental import pallas as pl
from jax.experimental.pallas import tpu as pltpu
from jax.sharding import PartitionSpec as P

M = 64
KN = 2
R = 128
DE = 896
DH = 128
SEQ_LEN = 2048
Z = 4
MESH = pl.DeviceIdType.MESH
F32 = jnp.float32
BF16 = jnp.bfloat16


def dot(a, b):
    return jnp.dot(a, b, preferred_element_type=F32)


def dot_nt(a, b):
    return lax.dot_general(a, b, (((1,), (1,)), ((), ())), preferred_element_type=F32)


def dot_tn(a, b):
    return lax.dot_general(a, b, (((0,), (0,)), ((), ())), preferred_element_type=F32)


def main_kernel(
    nseq, cap, heads,
    own_s, row_s, q_h, g_h, tab_h, kw_h, vw_h,
    dq_o, prev_o, back_o, reqs_o,
    tab, qv, gv, wp, wt, qf, qs, gs, tails,
    req, uos, reqs, reqs_s, uos_s, slot_s,
    send_a, recv_a, gat, kvt, grad_t, dq,
    sib_s, sib_r, own_p, s1_s, s1_r, s2_s, s2_r, res, send_b,
    loc_sem, id_sem, tail_sem, a_sem, f_sem, b_sem, e_sem, dqt_sem,
):
    spans = qs.shape[0]
    uses = spans * KN
    de_e = tab.shape[1]
    cols = heads * DH
    scale = 1.0 / math.sqrt(DH)
    s = lax.axis_index("seq")
    e = lax.axis_index("enc")
    z, core = e // 2, e % 2
    zp, zm, zo = (z + 1) % Z, (z + 3) % Z, (z + 2) % Z
    sib = (s, z * 2 + 1 - core)
    up, down = (s, zp * 2 + core), (s, zm * 2 + core)
    per_seq = SEQ_LEN // (spans * M)
    ring = min(per_seq, nseq)
    base = (s // ring) * ring
    following = (base + (s + 1) % ring, e)
    preceding = (base + (s + ring - 1) % ring, e)

    def remote(src, dst, sem, where):
        return pltpu.make_async_remote_copy(
            src_ref=src, dst_ref=dst, send_sem=sem.at[0], recv_sem=sem.at[1],
            device_id=where, device_id_type=MESH,
        )

    barrier = pltpu.get_barrier_semaphore()

    def greet(i, _):
        pl.semaphore_signal(barrier, inc=1, device_id=((s + i) % nseq, e), device_id_type=MESH)
        return 0

    lax.fori_loop(1, nseq, greet, 0)
    for where in (sib, up, down):
        pl.semaphore_signal(barrier, inc=1, device_id=where, device_id_type=MESH)

    local = [
        pltpu.make_async_copy(tab_h, tab, loc_sem.at[0]),
        pltpu.make_async_copy(q_h, qv, loc_sem.at[1]),
        pltpu.make_async_copy(g_h, gv, loc_sem.at[2]),
        pltpu.make_async_copy(kw_h.at[:, core], wp.at[0, :, :, pl.ds(0, cols)], loc_sem.at[3]),
        pltpu.make_async_copy(vw_h.at[:, core], wp.at[0, :, :, pl.ds(cols, cols)], loc_sem.at[4]),
        pltpu.make_async_copy(kw_h.at[:, 1 - core], wp.at[1, :, :, pl.ds(0, cols)], loc_sem.at[5]),
        pltpu.make_async_copy(vw_h.at[:, 1 - core], wp.at[1, :, :, pl.ds(cols, cols)], loc_sem.at[6]),
    ]
    for c in local:
        c.start()

    lane = lax.broadcasted_iota(jnp.int32, (1, 128), 1)
    lane_owner, lane_k = lane // cap, lane % cap
    count = jnp.zeros((1, 128), jnp.int32)
    rows = jnp.full((1, 128), -1, jnp.int32)
    use_of = jnp.zeros((1, 128), jnp.int32)
    owners = [own_s[u // KN, u % KN] for u in range(uses)]
    for u in range(uses):
        hit = lane_owner == owners[u]
        chosen = hit & (count == lane_k)
        rows = jnp.where(chosen, row_s[u // KN, u % KN], rows)
        use_of = jnp.where(chosen, u, use_of)
        count = count + hit.astype(jnp.int32)
        rank = jnp.int32(0)
        for v in range(u):
            rank = rank + (owners[v] == owners[u]).astype(jnp.int32)
        slot_s[u] = owners[u] * cap + rank
    req[...] = rows
    uos[...] = use_of
    reqs[s] = rows
    uos_copy = pltpu.make_async_copy(uos, uos_s, loc_sem.at[7])
    uos_copy.start()

    pl.semaphore_wait(barrier, nseq - 1 + 3)

    def id_copy(i):
        return remote(req, reqs.at[s], id_sem.at[i], ((s + i) % nseq, e))

    def send_ids(i, _):
        id_copy(i).start()
        return 0

    lax.fori_loop(1, nseq, send_ids, 0)
    q_tail = remote(q_h.at[pl.ds(0, M)], tails.at[0], tail_sem.at[0], preceding)
    g_tail = remote(g_h.at[pl.ds(0, M)], tails.at[1], tail_sem.at[1], preceding)

    def wait_ids(i, _):
        id_copy(i).wait_recv()
        return 0

    lax.fori_loop(1, nseq, wait_ids, 0)
    reqs_copy = pltpu.make_async_copy(reqs, reqs_s, loc_sem.at[8])
    reqs_copy.start()
    reqs_out = pltpu.make_async_copy(reqs, reqs_o, loc_sem.at[9])
    reqs_out.start()
    local[0].wait()
    reqs_copy.wait()

    def a_copy(i):
        peer = (s + i) % nseq
        return remote(send_a.at[peer], recv_a.at[s], a_sem.at[i], (peer, e))

    def send_rows(i, _):
        peer = (s + i) % nseq
        for k in range(cap):
            wanted = jnp.maximum(reqs_s[peer, 0, s * cap + k], 0)
            send_a[peer, k] = tab[wanted]
        a_copy(i).start()
        return 0

    lax.fori_loop(1, nseq, send_rows, 0)
    q_tail.start()
    g_tail.start()
    for k in range(cap):
        recv_a[s, k] = tab[jnp.maximum(reqs_s[s, 0, s * cap + k], 0)]

    for c in local[3:]:
        c.wait()

    def turn(b, _):
        at = pl.ds(pl.multiple_of(b * 128, 128), 128)
        wt[at, :] = wp[:, :, :, at].reshape(DE, 128).T
        return 0

    lax.fori_loop(0, 2 * cols // 128, turn, 0)
    local[1].wait()
    local[2].wait()
    q_tail.wait_recv()
    g_tail.wait_recv()
    inside = jnp.logical_and(s % per_seq != per_seq - 1, s != nseq - 1).astype(F32)
    for index, (source, target) in enumerate(((qv, qs), (gv, gs))):
        qf[pl.ds(0, spans * M), :] = source[...].astype(F32)
        qf[pl.ds(spans * M, M), :] = tails[index].astype(F32) * inside
        for c in range(spans):
            target[c] = qf[pl.ds(c * M + M - 1, M), :].astype(BF16)
    uos_copy.wait()

    def wait_rows(i, _):
        a_copy(i).wait_recv()
        return 0

    lax.fori_loop(1, nseq, wait_rows, 0)

    def f_up(j):
        return remote(gat.at[j, :, 0, z], gat.at[j, :, 0, z], f_sem.at[0, j], up)

    def f_down(j):
        return remote(gat.at[j, :, 0, z], gat.at[j, :, 0, z], f_sem.at[1, j], down)

    def f_half_up(j):
        return remote(gat.at[j, 0, 0, zm], gat.at[j, 0, 0, zm], f_sem.at[2, j], up)

    def f_half_down(j):
        return remote(gat.at[j, 1, 0, zp], gat.at[j, 1, 0, zp], f_sem.at[3, j], down)

    def f_sib(j, which, at):
        return remote(gat.at[j, :, 0, at], gat.at[j, :, 1, at], f_sem.at[4 + which, j], sib)

    def sibs(j):
        return [f_sib(j, 0, z), f_sib(j, 1, zm), f_sib(j, 2, zp), f_sib(j, 3, zo)]

    def b_sib(j):
        return remote(sib_s.at[j], sib_r.at[j], b_sem.at[0, j], sib)

    def b_one(j, d):
        return remote(s1_s.at[j, d], s1_r.at[j, d], b_sem.at[1 + d, j], (up, down)[d])

    def b_two(j, d):
        return remote(s2_s.at[j, d], s2_r.at[j, d], b_sem.at[3 + d, j], (up, down)[d])

    def forward_0(j):
        for t in range(KN):
            slot = slot_s[j * KN + t]
            gat[j, t, 0, z] = recv_a[slot // cap, slot % cap]
        f_up(j).start()
        f_down(j).start()
        f_sib(j, 0, z).start()

    def forward_1(j):
        f_up(j).wait_recv()
        f_half_up(j).start()
        f_sib(j, 1, zm).start()
        f_down(j).wait_recv()
        f_half_down(j).start()
        f_sib(j, 2, zp).start()

    def forward_2(j):
        f_half_up(j).wait_recv()
        f_half_down(j).wait_recv()
        f_sib(j, 3, zo).start()

    def forward_3(j):
        for c in sibs(j):
            c.wait_recv()

    def compute(j):
        blocks = jnp.concatenate([gat[j, t].reshape(DE, R) for t in range(KN)], axis=1)
        kvt[...] = dot(wt[...], blocks).astype(BF16)
        for h in range(heads):
            at = slice(h * DH, (h + 1) * DH)
            at_v = slice(cols + h * DH, cols + (h + 1) * DH)
            query, gradient = qs[j, :, at], gs[j, :, at]
            keys, values = kvt[at, :], kvt[at_v, :]
            scores = dot(query, keys) * scale
            powers = jnp.exp(scores - jnp.max(scores, axis=-1, keepdims=True))
            weights = powers / jnp.sum(powers, axis=-1, keepdims=True)
            rounded = weights.astype(BF16)
            product = dot(gradient, values)
            row_delta = jnp.sum(rounded.astype(F32) * product, axis=-1, keepdims=True)
            score_grad = (weights * (product - row_delta)).astype(BF16)
            dq[j, :, at] = (dot_nt(score_grad, keys) * scale).astype(BF16)
            grad_t[at, :] = (dot_tn(query, score_grad) * scale).astype(BF16)
            grad_t[at_v, :] = dot_tn(gradient, rounded).astype(BF16)
        other = dot(wp[1].reshape(DE // 2, 2 * cols), grad_t[...]).astype(BF16)
        for t in range(KN):
            sib_s[j, t] = other[:, t * R:(t + 1) * R].reshape(Z, de_e, R)
        b_sib(j).start()
        mine = dot(wp[0].reshape(DE // 2, 2 * cols), grad_t[...])
        for t in range(KN):
            own_p[j, t] = mine[:, t * R:(t + 1) * R].reshape(Z, de_e, R)

    def backward_1(j):
        b_sib(j).wait_recv()
        s1_s[j, 0] = (own_p[j, 0, zo] + sib_r[j, 0, zo].astype(F32)).astype(BF16)
        b_one(j, 0).start()
        s1_s[j, 1] = (own_p[j, 1, zo] + sib_r[j, 1, zo].astype(F32)).astype(BF16)
        b_one(j, 1).start()

    def backward_2(j):
        for d, at in ((0, zp), (1, zm)):
            b_one(j, d).wait_recv()
            for t in range(KN):
                term = own_p[j, t, at] + sib_r[j, t, at].astype(F32)
                if t == d:
                    term = term + s1_r[j, d].astype(F32)
                s2_s[j, d, t] = term.astype(BF16)
            b_two(j, d).start()

    def backward_3(j):
        for d in range(2):
            b_two(j, d).wait_recv()
        for t in range(KN):
            term = own_p[j, t, z] + sib_r[j, t, z].astype(F32)
            term = term + s2_r[j, 0, t].astype(F32) + s2_r[j, 1, t].astype(F32)
            res[j * KN + t] = term.astype(BF16)

    stages = (
        (0, forward_0), (1, forward_1), (2, forward_2), (5, backward_2), (6, backward_3),
        (3, forward_3), (3, compute), (4, backward_1),
    )

    def step(i, _):
        for offset, stage in stages:
            j = i - offset

            @pl.when(jnp.logical_and(j >= 0, j < spans))
            def _():
                stage(j)

        return 0

    lax.fori_loop(0, spans + 6, step, 0)

    dq_tail = remote(dq.at[spans - 1], prev_o, dqt_sem, following)
    dq_tail.start()
    dq_out = pltpu.make_async_copy(dq, dq_o, loc_sem.at[10])
    dq_out.start()

    def e_copy(i):
        peer = (s + i) % nseq
        return remote(send_b.at[peer], back_o.at[s], e_sem.at[i], (peer, e))

    def send_terms(i, _):
        peer = (s + i) % nseq
        for k in range(cap):
            send_b[peer, k] = res[uos_s[0, peer * cap + k]]
        e_copy(i).start()
        return 0

    lax.fori_loop(1, nseq, send_terms, 0)
    for k in range(cap):
        send_b[s, k] = res[uos_s[0, s * cap + k]]
    own_back = pltpu.make_async_copy(send_b.at[s], back_o.at[s], loc_sem.at[11])
    own_back.start()

    def drain(j, _):
        for c in [f_up(j), f_down(j), f_half_up(j), f_half_down(j)] + sibs(j):
            c.wait_send()
        for c in (b_sib(j), b_one(j, 0), b_one(j, 1), b_two(j, 0), b_two(j, 1)):
            c.wait_send()
        return 0

    lax.fori_loop(0, spans, drain, 0)

    def drain_peers(i, _):
        id_copy(i).wait_send()
        a_copy(i).wait_send()
        e_copy(i).wait()
        return 0

    lax.fori_loop(1, nseq, drain_peers, 0)
    q_tail.wait_send()
    g_tail.wait_send()
    dq_tail.wait()
    dq_out.wait()
    own_back.wait()
    reqs_out.wait()


def last_kernel(nseq, cap, reqs_s, back, dq, prev, dquery_o, dtable_o, shift):
    s = lax.axis_index("seq")
    rows = dquery_o.shape[0]
    per_seq = SEQ_LEN // rows
    shift[pl.ds(0, M), :] = prev[...].astype(F32) * (s % per_seq != 0).astype(F32)
    shift[pl.ds(M, rows), :] = dq[...].reshape(rows, dq.shape[2]).astype(F32)
    dquery_o[...] = shift[pl.ds(1, rows), :].astype(BF16)
    dtable_o[...] = jnp.zeros_like(dtable_o)

    def add(i, _):
        row = reqs_s[i // cap, 0, s * cap + i % cap]

        @pl.when(row >= 0)
        def _():
            dtable_o[row] += back[i // cap, i % cap].astype(F32)

        return 0

    lax.fori_loop(0, nseq * cap, add, 0)


def local(queries, out_grad, enc_table, key_weight, value_weight, neighbour_owner, neighbour_row):
    nseq = lax.axis_size("seq")
    tok_rows, cols = queries.shape
    heads = cols // DH
    spans = tok_rows // M
    uses = spans * KN
    cap = max(2, uses // nseq)
    blocks, de_e, _ = enc_table.shape
    any_spec = pl.BlockSpec(memory_space=pl.ANY)
    smem = pl.BlockSpec(memory_space=pltpu.SMEM)
    vmem = pl.BlockSpec(memory_space=pltpu.VMEM)
    piece = (de_e, R)
    dma = pltpu.SemaphoreType.DMA
    dq, prev, back, reqs = pl.pallas_call(
        functools.partial(main_kernel, nseq, cap, heads),
        out_shape=(
            jax.ShapeDtypeStruct((spans, M, cols), BF16),
            jax.ShapeDtypeStruct((M, cols), BF16),
            jax.ShapeDtypeStruct((nseq, cap) + piece, BF16),
            jax.ShapeDtypeStruct((nseq, 1, 128), jnp.int32),
        ),
        in_specs=[smem, smem] + [any_spec] * 5,
        out_specs=(any_spec,) * 4,
        scratch_shapes=[
            pltpu.VMEM((blocks,) + piece, BF16),
            pltpu.VMEM((tok_rows, cols), BF16),
            pltpu.VMEM((tok_rows, cols), BF16),
            pltpu.VMEM((2, Z, de_e, 2 * cols), BF16),
            pltpu.VMEM((2 * cols, DE), BF16),
            pltpu.VMEM((tok_rows + M, cols), F32),
            pltpu.VMEM((spans, M, cols), BF16),
            pltpu.VMEM((spans, M, cols), BF16),
            pltpu.VMEM((2, M, cols), BF16),
            pltpu.VMEM((1, 128), jnp.int32),
            pltpu.VMEM((1, 128), jnp.int32),
            pltpu.VMEM((nseq, 1, 128), jnp.int32),
            pltpu.SMEM((nseq, 1, 128), jnp.int32),
            pltpu.SMEM((1, 128), jnp.int32),
            pltpu.SMEM((uses,), jnp.int32),
            pltpu.VMEM((nseq, cap) + piece, BF16),
            pltpu.VMEM((nseq, cap) + piece, BF16),
            pltpu.VMEM((spans, KN, 2, Z) + piece, BF16),
            pltpu.VMEM((2 * cols, KN * R), BF16),
            pltpu.VMEM((2 * cols, KN * R), BF16),
            pltpu.VMEM((spans, M, cols), BF16),
            pltpu.VMEM((spans, KN, Z) + piece, BF16),
            pltpu.VMEM((spans, KN, Z) + piece, BF16),
            pltpu.VMEM((spans, KN, Z) + piece, F32),
            pltpu.VMEM((spans, 2) + piece, BF16),
            pltpu.VMEM((spans, 2) + piece, BF16),
            pltpu.VMEM((spans, 2, KN) + piece, BF16),
            pltpu.VMEM((spans, 2, KN) + piece, BF16),
            pltpu.VMEM((uses,) + piece, BF16),
            pltpu.VMEM((nseq, cap) + piece, BF16),
            dma((12,)),
            dma((nseq, 2)),
            dma((2, 2)),
            dma((nseq, 2)),
            dma((8, spans, 2)),
            dma((5, spans, 2)),
            dma((nseq, 2)),
            dma((2,)),
        ],
        compiler_params=pltpu.CompilerParams(
            collective_id=0, has_side_effects=True, vmem_limit_bytes=56 * 2**20
        ),
    )(
        neighbour_owner, neighbour_row, queries, out_grad, enc_table,
        key_weight.reshape(Z, 2, de_e, cols), value_weight.reshape(Z, 2, de_e, cols),
    )
    return pl.pallas_call(
        functools.partial(last_kernel, nseq, cap),
        out_shape=(
            jax.ShapeDtypeStruct((tok_rows, cols), BF16),
            jax.ShapeDtypeStruct((blocks,) + piece, F32),
        ),
        in_specs=[smem, vmem, vmem, vmem],
        out_specs=(vmem, vmem),
        scratch_shapes=[pltpu.VMEM((tok_rows + M, cols), F32)],
        compiler_params=pltpu.CompilerParams(vmem_limit_bytes=32 * 2**20),
    )(reqs, back, dq, prev)


def solution(mesh):
    in_specs = (
        P("seq", "enc"),
        P("seq", "enc"),
        P("seq", "enc", None),
        P(None, "enc"),
        P(None, "enc"),
        P("seq", None),
        P("seq", None),
    )
    out_specs = (P("seq", "enc"), P("seq", "enc", None))
    return jax.shard_map(local, mesh=mesh, in_specs=in_specs, out_specs=out_specs, check_vma=False)
```

time: 670 us -> 124 us (0.19)
  blocking collectives: 270 us -> 0 us
  waiting for transfers between devices: 235 us -> 0 us
  Pallas kernels: 0 us -> 117 us
  local copies, waits for them, and re-layouts: 88.6 us -> 6.44 us
  matrix products: 42.6 us -> 0 us
  starting transfers between devices: 17.8 us -> 0 us
  other arithmetic: 12.4 us -> 0 us
    all_to_all x3 -> x0, blocking collectives: 270 us -> none  [the longest x1 169 us: local(): lax.all_to_all(placed.reshape(slot_total, enc_count, column_width, R), 's...]
    all_to_all x2 -> x0, waiting for transfers between devices: 228 us -> none  [the longest x1 154 us: local(): lax.all_to_all(lax.all_to_all(placed.reshape(slot_total, enc_count, colum...]
    pallas_call x0 -> x2, Pallas kernels: none -> 117 us  [the longest x1 113 us: local(): pl.pallas_call(functools.partial(main_kernel, nseq, cap, heads), out_shap...]
    dot_general x9 -> x0, matrix products: 42.6 us -> none  [the longest x1 7.88 us: local(): jnp.einsum('urc,dc->udr', both_grads, joint_weight, preferred_element_typ...]
    all_to_all x6 -> x0, local copies, waits for them, and re-layouts: 25 us -> none  [the longest x1 11.8 us: local(): lax.all_to_all(placed.reshape(slot_total, enc_count, column_width, R), 's...]
    reshape x7 -> x0, local copies, waits for them, and re-layouts: 24.9 us -> none  [the longest x2 8.45 us: local(): key_grad.reshape(use_count, R, head_columns)]
    scatter x2 -> x0, local copies, waits for them, and re-layouts: 14.9 us -> none  [the longest x1 14.2 us: local(): jnp.zeros((slot_total, DE, R), jnp.float32).at[slot_index]]
    all_to_all x2 -> x0, starting transfers between devices: 14.3 us -> none  [the longest x1 8.77 us: local(): lax.all_to_all(lax.all_to_all(placed.reshape(slot_total, enc_count, colum...]
  transfers between devices with their start and end apart: 4 -> 0, of which waited for: 4 -> 0; matrix products, arithmetic and copies ran while one was open for 1% -> 0% of each run, Pallas kernels for 0% -> 0%
where the time goes in v1:
time: 124 us
  Pallas kernels  117 us (94%)
  local copies, waits for them, and re-layouts  6.44 us (5%)
    pallas_call x1, Pallas kernels, local(): pl.pallas_call(functools.partial(main_kernel, nseq, cap, heads), out_shap...  113 us
    unnamed x10, local copies, waits for them, and re-layouts  6.44 us
    pallas_call x1, Pallas kernels, local(): pl.pallas_call(functools.partial(last_kernel, nseq, cap), out_shape=(jax....  3.86 us

profile of v1, /device:TPU:32, one launch (start us, length us, event | category | flops | bytes accessed | tf_op | source)
XLA Modules:
  0.0 124.0 jit_solution(1216669960469136861)
XLA Ops:
  0.6 1.3 %copy.9.own_s = s32[8,2]{1,0:T(8,128)} copy(s32[8,2]{0,1:T(2,128)} %param.12) | data formatting | bytes 128 | tf_op args[5]
  2.0 1.3 %copy.10.row_s = s32[8,2]{1,0:T(8,128)} copy(s32[8,2]{0,1:T(2,128)} %param.13) | data formatting | bytes 128 | tf_op args[6]
  3.3 113.1 %shard_map.86 = (bf16[8,64,512]{2,1,0:T(8,128)(2,1)}, bf16[64,512]{1,0:T(8,128)(2,1)}, bf16[16,2,112,128]{3,2,1,0:T(8,128)(2,1)}, s32[16,1,128]{2,1,0:T(1,128)}) custom-call(s32[8,2]{1,0:T(8,128)} %copy.9.own_s, s32[8,2]{1,0:T(8,128)} %copy.10.row_s, bf16[512,512]{1,0:T(8,128)(2,1)} %q_h.1, bf16[512,512]{1,0:T(8,128)(2,1)} %g_h.1, ...), custom_call_target="tpu_custom_call" | custom-call | tf_op jit(solution)/shard_map/pallas_call | solution.py:382
  116.4 0.0 copy-start
  116.4 1.2 copy-done
  117.6 0.0 copy-start.1
  117.6 1.0 copy-done.1
  118.7 0.0 copy-start.2
  118.7 0.8 copy-done.2
  119.5 0.0 copy-start.3
  119.5 0.7 copy-done.3
  120.2 3.9 %shard_map.87 = (bf16[512,512]{1,0:T(8,128)(2,1)}, f32[64,112,128]{2,1,0:T(8,128)}) custom-call(s32[16,1,128]{2,1,0:T(1,128)S(1)} %copy-done.3, bf16[16,2,112,128]{3,2,1,0:T(8,128)(2,1)S(1)} %copy-done, bf16[8,64,512]{2,1,0:T(8,128)(2,1)S(1)} %copy-done.1, bf16[64,512]{1,0:T(8,128)(2,1)S(1)} %copy-done.2), custom_call_target="tpu_custom_call" | custom-call | tf_op jit(solution)/shard_map/pallas_call | solution.py:439
Async XLA Ops:
  116.4 1.2 copy-start
  117.6 1.0 copy-start.1
  118.7 0.8 copy-start.2
  119.5 0.7 copy-start.3

commit v2 on v1

--- a/solution.py
+++ b/solution.py
@@ -28,18 +28,14 @@
     return lax.dot_general(a, b, (((1,), (1,)), ((), ())), preferred_element_type=F32)
 
 
-def dot_tn(a, b):
-    return lax.dot_general(a, b, (((0,), (0,)), ((), ())), preferred_element_type=F32)
-
-
 def main_kernel(
     nseq, cap, heads,
-    own_s, row_s, q_h, g_h, tab_h, kw_h, vw_h,
+    own_h, row_h, q_h, g_h, tab_h, kw_h, vw_h,
     dq_o, prev_o, back_o, reqs_o,
-    tab, qv, gv, wp, wt, qf, qs, gs, tails,
+    own_s, row_s, tab, qv, gv, wp, wt, qf, qs, gs, qt, gt, tails,
     req, uos, reqs, reqs_s, uos_s, slot_s,
     send_a, recv_a, gat, kvt, grad_t, dq,
-    sib_s, sib_r, own_p, s1_s, s1_r, s2_s, s2_r, res, send_b,
+    terms, sib_r, s1_s, s1_r, s2_s, s2_r, res, send_b,
     loc_sem, id_sem, tail_sem, a_sem, f_sem, b_sem, e_sem, dqt_sem,
 ):
     spans = qs.shape[0]
@@ -75,6 +71,12 @@
     for where in (sib, up, down):
         pl.semaphore_signal(barrier, inc=1, device_id=where, device_id_type=MESH)
 
+    ids_in = [
+        pltpu.make_async_copy(own_h, own_s, loc_sem.at[12]),
+        pltpu.make_async_copy(row_h, row_s, loc_sem.at[13]),
+    ]
+    for c in ids_in:
+        c.start()
     local = [
         pltpu.make_async_copy(tab_h, tab, loc_sem.at[0]),
         pltpu.make_async_copy(q_h, qv, loc_sem.at[1]),
@@ -87,16 +89,19 @@
     for c in local:
         c.start()
 
+    for c in ids_in:
+        c.wait()
+
     lane = lax.broadcasted_iota(jnp.int32, (1, 128), 1)
     lane_owner, lane_k = lane // cap, lane % cap
     count = jnp.zeros((1, 128), jnp.int32)
     rows = jnp.full((1, 128), -1, jnp.int32)
     use_of = jnp.zeros((1, 128), jnp.int32)
-    owners = [own_s[u // KN, u % KN] for u in range(uses)]
+    owners = [own_s[u % KN, u // KN] for u in range(uses)]
     for u in range(uses):
         hit = lane_owner == owners[u]
         chosen = hit & (count == lane_k)
-        rows = jnp.where(chosen, row_s[u // KN, u % KN], rows)
+        rows = jnp.where(chosen, row_s[u % KN, u // KN], rows)
         use_of = jnp.where(chosen, u, use_of)
         count = count + hit.astype(jnp.int32)
         rank = jnp.int32(0)
@@ -122,6 +127,30 @@
     q_tail = remote(q_h.at[pl.ds(0, M)], tails.at[0], tail_sem.at[0], preceding)
     g_tail = remote(g_h.at[pl.ds(0, M)], tails.at[1], tail_sem.at[1], preceding)
 
+    q_tail.start()
+    g_tail.start()
+
+    for c in local[3:]:
+        c.wait()
+
+    def turn(b, _):
+        at = pl.ds(pl.multiple_of(b * 128, 128), 128)
+        wt[at, :] = wp[:, :, :, at].reshape(DE, 128).T
+        return 0
+
+    lax.fori_loop(0, 2 * cols // 128, turn, 0)
+
+    def shift(index, c):
+        moved = qf[index, pl.ds(c * M + M - 1, M), :].astype(BF16)
+        (qs, gs)[index][c] = moved
+        (qt, gt)[index][c] = moved.T
+
+    for index, source in enumerate((qv, gv)):
+        local[1 + index].wait()
+        qf[index, pl.ds(0, spans * M), :] = source[...].astype(F32)
+        for c in range(spans - 1):
+            shift(index, c)
+
     def wait_ids(i, _):
         id_copy(i).wait_recv()
         return 0
@@ -147,30 +176,15 @@
         return 0
 
     lax.fori_loop(1, nseq, send_rows, 0)
-    q_tail.start()
-    g_tail.start()
     for k in range(cap):
         recv_a[s, k] = tab[jnp.maximum(reqs_s[s, 0, s * cap + k], 0)]
 
-    for c in local[3:]:
-        c.wait()
-
-    def turn(b, _):
-        at = pl.ds(pl.multiple_of(b * 128, 128), 128)
-        wt[at, :] = wp[:, :, :, at].reshape(DE, 128).T
-        return 0
-
-    lax.fori_loop(0, 2 * cols // 128, turn, 0)
-    local[1].wait()
-    local[2].wait()
     q_tail.wait_recv()
     g_tail.wait_recv()
     inside = jnp.logical_and(s % per_seq != per_seq - 1, s != nseq - 1).astype(F32)
-    for index, (source, target) in enumerate(((qv, qs), (gv, gs))):
-        qf[pl.ds(0, spans * M), :] = source[...].astype(F32)
-        qf[pl.ds(spans * M, M), :] = tails[index].astype(F32) * inside
-        for c in range(spans):
-            target[c] = qf[pl.ds(c * M + M - 1, M), :].astype(BF16)
+    for index in range(2):
+        qf[index, pl.ds(spans * M, M), :] = tails[index].astype(F32) * inside
+        shift(index, spans - 1)
     uos_copy.wait()
 
     def wait_rows(i, _):
@@ -198,7 +212,7 @@
         return [f_sib(j, 0, z), f_sib(j, 1, zm), f_sib(j, 2, zp), f_sib(j, 3, zo)]
 
     def b_sib(j):
-        return remote(sib_s.at[j], sib_r.at[j], b_sem.at[0, j], sib)
+        return remote(terms.at[1, j], sib_r.at[j], b_sem.at[0, j], sib)
 
     def b_one(j, d):
         return remote(s1_s.at[j, d], s1_r.at[j, d], b_sem.at[1 + d, j], (up, down)[d])
@@ -231,44 +245,57 @@
         for c in sibs(j):
             c.wait_recv()
 
-    def compute(j):
-        blocks = jnp.concatenate([gat[j, t].reshape(DE, R) for t in range(KN)], axis=1)
-        kvt[...] = dot(wt[...], blocks).astype(BF16)
-        for h in range(heads):
-            at = slice(h * DH, (h + 1) * DH)
-            at_v = slice(cols + h * DH, cols + (h + 1) * DH)
-            query, gradient = qs[j, :, at], gs[j, :, at]
-            keys, values = kvt[at, :], kvt[at_v, :]
-            scores = dot(query, keys) * scale
-            powers = jnp.exp(scores - jnp.max(scores, axis=-1, keepdims=True))
-            weights = powers / jnp.sum(powers, axis=-1, keepdims=True)
-            rounded = weights.astype(BF16)
-            product = dot(gradient, values)
-            row_delta = jnp.sum(rounded.astype(F32) * product, axis=-1, keepdims=True)
-            score_grad = (weights * (product - row_delta)).astype(BF16)
-            dq[j, :, at] = (dot_nt(score_grad, keys) * scale).astype(BF16)
-            grad_t[at, :] = (dot_tn(query, score_grad) * scale).astype(BF16)
-            grad_t[at_v, :] = dot_tn(gradient, rounded).astype(BF16)
-        other = dot(wp[1].reshape(DE // 2, 2 * cols), grad_t[...]).astype(BF16)
-        for t in range(KN):
-            sib_s[j, t] = other[:, t * R:(t + 1) * R].reshape(Z, de_e, R)
-        b_sib(j).start()
-        mine = dot(wp[0].reshape(DE // 2, 2 * cols), grad_t[...])
-        for t in range(KN):
-            own_p[j, t] = mine[:, t * R:(t + 1) * R].reshape(Z, de_e, R)
+    def project(j):
+        half = cols
+
+        def some(b, _):
+            at = pl.ds(pl.multiple_of(b * half, half), half)
+            blocks = jnp.concatenate([gat[j, t].reshape(DE, R) for t in range(KN)], axis=1)
+            kvt[at, :] = dot(wt[at, :], blocks).astype(BF16)
+            return 0
+
+        lax.fori_loop(0, 2, some, 0)
+
+    def attend(j):
+        hs = range(heads)
+        at = [slice(h * DH, (h + 1) * DH) for h in hs]
+        at_v = [slice(cols + h * DH, cols + (h + 1) * DH) for h in hs]
+        scores = [dot(qs[j, :, at[h]], kvt[at[h], :]) * (scale * math.log2(math.e)) for h in hs]
+        product = [dot(gs[j, :, at[h]], kvt[at_v[h], :]) for h in hs]
+        powers = [jnp.exp2(x - jnp.max(x, axis=-1, keepdims=True)) for x in scores]
+        weights = [x * (1.0 / jnp.sum(x, axis=-1, keepdims=True)) for x in powers]
+        rounded = [x.astype(BF16) for x in weights]
+        row_delta = [
+            jnp.sum(x.astype(F32) * y, axis=-1, keepdims=True) for x, y in zip(rounded, product)
+        ]
+        score_grad = [(x * (y - d)).astype(BF16) for x, y, d in zip(weights, product, row_delta)]
+        for h in hs:
+            grad_t[at_v[h], :] = dot(gt[j, at[h], :], rounded[h]).astype(BF16)
+        for h in hs:
+            dq[j, :, at[h]] = (dot_nt(score_grad[h], kvt[at[h], :]) * scale).astype(BF16)
+            grad_t[at[h], :] = (dot(qt[j, at[h], :], score_grad[h]) * scale).astype(BF16)
+        for side in (1, 0):
+            term = dot(wp[side].reshape(DE // 2, 2 * cols), grad_t[...]).astype(BF16)
+            for t in range(KN):
+                terms[side, j, t] = term[:, t * R:(t + 1) * R].reshape(Z, de_e, R)
+            if side == 1:
+                b_sib(j).start()
+
+    def both(j, t, at):
+        return terms[0, j, t, at].astype(F32) + sib_r[j, t, at].astype(F32)
 
     def backward_1(j):
         b_sib(j).wait_recv()
-        s1_s[j, 0] = (own_p[j, 0, zo] + sib_r[j, 0, zo].astype(F32)).astype(BF16)
+        s1_s[j, 0] = both(j, 0, zo).astype(BF16)
         b_one(j, 0).start()
-        s1_s[j, 1] = (own_p[j, 1, zo] + sib_r[j, 1, zo].astype(F32)).astype(BF16)
+        s1_s[j, 1] = both(j, 1, zo).astype(BF16)
         b_one(j, 1).start()
 
     def backward_2(j):
         for d, at in ((0, zp), (1, zm)):
             b_one(j, d).wait_recv()
             for t in range(KN):
-                term = own_p[j, t, at] + sib_r[j, t, at].astype(F32)
+                term = both(j, t, at)
                 if t == d:
                     term = term + s1_r[j, d].astype(F32)
                 s2_s[j, d, t] = term.astype(BF16)
@@ -278,13 +305,12 @@
         for d in range(2):
             b_two(j, d).wait_recv()
         for t in range(KN):
-            term = own_p[j, t, z] + sib_r[j, t, z].astype(F32)
-            term = term + s2_r[j, 0, t].astype(F32) + s2_r[j, 1, t].astype(F32)
+            term = both(j, t, z) + s2_r[j, 0, t].astype(F32) + s2_r[j, 1, t].astype(F32)
             res[j * KN + t] = term.astype(BF16)
 
     stages = (
-        (0, forward_0), (1, forward_1), (2, forward_2), (5, backward_2), (6, backward_3),
-        (3, forward_3), (3, compute), (4, backward_1),
+        (0, forward_0), (1, forward_1), (2, forward_2), (3, forward_3), (3, project),
+        (4, backward_1), (5, backward_2), (6, backward_3), (3, attend),
     )
 
     def step(i, _):
@@ -345,25 +371,44 @@
     reqs_out.wait()
 
 
-def last_kernel(nseq, cap, reqs_s, back, dq, prev, dquery_o, dtable_o, shift):
+def last_kernel(
+    nseq, cap, reqs_h, back_h, dq_h, prev_h, dquery_o, dtable_o,
+    reqs_s, back, dq, prev, shift, moved, total, sem,
+):
+    ins = [
+        pltpu.make_async_copy(reqs_h, reqs_s, sem.at[0]),
+        pltpu.make_async_copy(dq_h, dq, sem.at[1]),
+        pltpu.make_async_copy(prev_h, prev, sem.at[2]),
+        pltpu.make_async_copy(back_h, back, sem.at[3]),
+    ]
+    for c in ins:
+        c.start()
+    total[...] = jnp.zeros_like(total)
     s = lax.axis_index("seq")
     rows = dquery_o.shape[0]
     per_seq = SEQ_LEN // rows
+    for c in ins:
+        c.wait()
+
+    def add(i, _):
+        row = reqs_s[i // cap, 0, s * cap + i % cap]
+
+        @pl.when(row >= 0)
+        def _():
+            total[row] += back[i // cap, i % cap].astype(F32)
+
+        return 0
+
+    lax.fori_loop(0, nseq * cap, add, 0)
+    table_out = pltpu.make_async_copy(total, dtable_o, sem.at[4])
+    table_out.start()
     shift[pl.ds(0, M), :] = prev[...].astype(F32) * (s % per_seq != 0).astype(F32)
     shift[pl.ds(M, rows), :] = dq[...].reshape(rows, dq.shape[2]).astype(F32)
-    dquery_o[...] = shift[pl.ds(1, rows), :].astype(BF16)
-    dtable_o[...] = jnp.zeros_like(dtable_o)
-
-    def add(i, _):
-        row = reqs_s[i // cap, 0, s * cap + i % cap]
-
-        @pl.when(row >= 0)
-        def _():
-            dtable_o[row] += back[i // cap, i % cap].astype(F32)
-
-        return 0
-
-    lax.fori_loop(0, nseq * cap, add, 0)
+    moved[...] = shift[pl.ds(1, rows), :].astype(BF16)
+    query_out = pltpu.make_async_copy(moved, dquery_o, sem.at[5])
+    query_out.start()
+    table_out.wait()
+    query_out.wait()
 
 
 def local(queries, out_grad, enc_table, key_weight, value_weight, neighbour_owner, neighbour_row):
@@ -375,8 +420,6 @@
     cap = max(2, uses // nseq)
     blocks, de_e, _ = enc_table.shape
     any_spec = pl.BlockSpec(memory_space=pl.ANY)
-    smem = pl.BlockSpec(memory_space=pltpu.SMEM)
-    vmem = pl.BlockSpec(memory_space=pltpu.VMEM)
     piece = (de_e, R)
     dma = pltpu.SemaphoreType.DMA
     dq, prev, back, reqs = pl.pallas_call(
@@ -387,17 +430,21 @@
             jax.ShapeDtypeStruct((nseq, cap) + piece, BF16),
             jax.ShapeDtypeStruct((nseq, 1, 128), jnp.int32),
         ),
-        in_specs=[smem, smem] + [any_spec] * 5,
+        in_specs=[any_spec] * 7,
         out_specs=(any_spec,) * 4,
         scratch_shapes=[
+            pltpu.SMEM((KN, spans), jnp.int32),
+            pltpu.SMEM((KN, spans), jnp.int32),
             pltpu.VMEM((blocks,) + piece, BF16),
             pltpu.VMEM((tok_rows, cols), BF16),
             pltpu.VMEM((tok_rows, cols), BF16),
             pltpu.VMEM((2, Z, de_e, 2 * cols), BF16),
             pltpu.VMEM((2 * cols, DE), BF16),
-            pltpu.VMEM((tok_rows + M, cols), F32),
+            pltpu.VMEM((2, tok_rows + M, cols), F32),
             pltpu.VMEM((spans, M, cols), BF16),
             pltpu.VMEM((spans, M, cols), BF16),
+            pltpu.VMEM((spans, cols, M), BF16),
+            pltpu.VMEM((spans, cols, M), BF16),
             pltpu.VMEM((2, M, cols), BF16),
             pltpu.VMEM((1, 128), jnp.int32),
             pltpu.VMEM((1, 128), jnp.int32),
@@ -411,16 +458,15 @@
             pltpu.VMEM((2 * cols, KN * R), BF16),
             pltpu.VMEM((2 * cols, KN * R), BF16),
             pltpu.VMEM((spans, M, cols), BF16),
+            pltpu.VMEM((2, spans, KN, Z) + piece, BF16),
             pltpu.VMEM((spans, KN, Z) + piece, BF16),
-            pltpu.VMEM((spans, KN, Z) + piece, BF16),
-            pltpu.VMEM((spans, KN, Z) + piece, F32),
             pltpu.VMEM((spans, 2) + piece, BF16),
             pltpu.VMEM((spans, 2) + piece, BF16),
             pltpu.VMEM((spans, 2, KN) + piece, BF16),
             pltpu.VMEM((spans, 2, KN) + piece, BF16),
             pltpu.VMEM((uses,) + piece, BF16),
             pltpu.VMEM((nseq, cap) + piece, BF16),
-            dma((12,)),
+            dma((14,)),
             dma((nseq, 2)),
             dma((2, 2)),
             dma((nseq, 2)),
@@ -433,7 +479,7 @@
             collective_id=0, has_side_effects=True, vmem_limit_bytes=56 * 2**20
         ),
     )(
-        neighbour_owner, neighbour_row, queries, out_grad, enc_table,
+        neighbour_owner.T, neighbour_row.T, queries, out_grad, enc_table,
         key_weight.reshape(Z, 2, de_e, cols), value_weight.reshape(Z, 2, de_e, cols),
     )
     return pl.pallas_call(
@@ -442,10 +488,19 @@
             jax.ShapeDtypeStruct((tok_rows, cols), BF16),
             jax.ShapeDtypeStruct((blocks,) + piece, F32),
         ),
-        in_specs=[smem, vmem, vmem, vmem],
-        out_specs=(vmem, vmem),
-        scratch_shapes=[pltpu.VMEM((tok_rows + M, cols), F32)],
-        compiler_params=pltpu.CompilerParams(vmem_limit_bytes=32 * 2**20),
+        in_specs=[any_spec] * 4,
+        out_specs=(any_spec,) * 2,
+        scratch_shapes=[
+            pltpu.SMEM((nseq, 1, 128), jnp.int32),
+            pltpu.VMEM((nseq, cap) + piece, BF16),
+            pltpu.VMEM((spans, M, cols), BF16),
+            pltpu.VMEM((M, cols), BF16),
+            pltpu.VMEM((tok_rows + M, cols), F32),
+            pltpu.VMEM((tok_rows, cols), BF16),
+            pltpu.VMEM((blocks,) + piece, F32),
+            dma((6,)),
+        ],
+        compiler_params=pltpu.CompilerParams(vmem_limit_bytes=60 * 2**20),
     )(reqs, back, dq, prev)
 
 

time: 124 us -> 93.5 us (0.75)
  Pallas kernels: 117 us -> 91.9 us
  local copies, waits for them, and re-layouts: 6.44 us -> 0 us
    pallas_call x1, Pallas kernels: 113 us -> 87.8 us  [local(): pl.pallas_call(functools.partial(main_kernel, nseq, cap, heads), out_shap...]
    unnamed x10 -> x0, local copies, waits for them, and re-layouts: 6.44 us -> none
where the time goes in v2:
time: 93.5 us; the launch traced here: 92.6 us
  Pallas kernels  91.9 us (98%)
    pallas_call x1, Pallas kernels, local(): pl.pallas_call(functools.partial(main_kernel, nseq, cap, heads), out_shap...  87.8 us
    pallas_call x1, Pallas kernels, local(): pl.pallas_call(functools.partial(last_kernel, nseq, cap), out_shape=(jax....  4.16 us

profile of v2, /device:TPU:32, one launch (start us, length us, event | category | flops | bytes accessed | tf_op | source)
XLA Modules:
  0.0 92.6 jit_solution(14173040710834937702)
XLA Ops:
  0.6 87.8 %shard_map.86 = (bf16[8,64,512]{2,1,0:T(8,128)(2,1)}, bf16[64,512]{1,0:T(8,128)(2,1)}, bf16[16,2,112,128]{3,2,1,0:T(8,128)(2,1)}, s32[16,1,128]{2,1,0:T(1,128)}) custom-call(s32[2,8]{1,0:T(2,128)} %bitcast.6, s32[2,8]{1,0:T(2,128)} %bitcast.7, bf16[512,512]{1,0:T(8,128)(2,1)} %q_h.1, bf16[512,512]{1,0:T(8,128)(2,1)} %g_h.1, bf16[64,112,128]{2,1,0:T(8,128)(2,1)} %tab_h.1, ...), custom_call_target="tpu_custom_call" | custom-call | tf_op jit(solution)/shard_map/pallas_call | solution.py:425
  88.4 4.2 %shard_map.87 = (bf16[512,512]{1,0:T(8,128)(2,1)}, f32[64,112,128]{2,1,0:T(8,128)}) custom-call(s32[16,1,128]{2,1,0:T(1,128)} %get-tuple-element.6.reqs_h, bf16[16,2,112,128]{3,2,1,0:T(8,128)(2,1)} %get-tuple-element.7.back_h, bf16[8,64,512]{2,1,0:T(8,128)(2,1)} %get-tuple-element.8.dq_h, bf16[64,512]{1,0:T(8,128)(2,1)} %get-tuple-element.9.prev_h), custom_call_target="tpu_custom_call" | custom-call | tf_op jit(solution)/shard_map/pallas_call | solution.py:485

commit v3 on v2

--- a/solution.py
+++ b/solution.py
@@ -205,11 +205,11 @@
     def f_half_down(j):
         return remote(gat.at[j, 1, 0, zp], gat.at[j, 1, 0, zp], f_sem.at[3, j], down)
 
-    def f_sib(j, which, at):
-        return remote(gat.at[j, :, 0, at], gat.at[j, :, 1, at], f_sem.at[4 + which, j], sib)
+    def f_sib(j):
+        return remote(gat.at[j, :, 0], gat.at[j, :, 1], f_sem.at[4, j], sib)
 
     def sibs(j):
-        return [f_sib(j, 0, z), f_sib(j, 1, zm), f_sib(j, 2, zp), f_sib(j, 3, zo)]
+        return [f_sib(j)]
 
     def b_sib(j):
         return remote(terms.at[1, j], sib_r.at[j], b_sem.at[0, j], sib)
@@ -226,20 +226,17 @@
             gat[j, t, 0, z] = recv_a[slot // cap, slot % cap]
         f_up(j).start()
         f_down(j).start()
-        f_sib(j, 0, z).start()
 
     def forward_1(j):
         f_up(j).wait_recv()
         f_half_up(j).start()
-        f_sib(j, 1, zm).start()
         f_down(j).wait_recv()
         f_half_down(j).start()
-        f_sib(j, 2, zp).start()
 
     def forward_2(j):
         f_half_up(j).wait_recv()
         f_half_down(j).wait_recv()
-        f_sib(j, 3, zo).start()
+        f_sib(j).start()
 
     def forward_3(j):
         for c in sibs(j):
@@ -308,10 +305,7 @@
             term = both(j, t, z) + s2_r[j, 0, t].astype(F32) + s2_r[j, 1, t].astype(F32)
             res[j * KN + t] = term.astype(BF16)
 
-    stages = (
-        (0, forward_0), (1, forward_1), (2, forward_2), (3, forward_3), (3, project),
-        (4, backward_1), (5, backward_2), (6, backward_3), (3, attend),
-    )
+    stages = ((0, forward_0), (4, forward_2), (2, forward_1), (5, forward_3), (5, project), (10, backward_3), (8, backward_2), (6, backward_1), (5, attend))
 
     def step(i, _):
         for offset, stage in stages:
@@ -323,7 +317,7 @@
 
         return 0
 
-    lax.fori_loop(0, spans + 6, step, 0)
+    lax.fori_loop(0, spans + 10, step, 0)
 
     dq_tail = remote(dq.at[spans - 1], prev_o, dqt_sem, following)
     dq_tail.start()

time: 93.5 us -> 87.1 us (0.932)
  Pallas kernels: 91.9 us -> 85.2 us
    pallas_call x1, Pallas kernels: 87.8 us -> 81.1 us  [local(): pl.pallas_call(functools.partial(main_kernel, nseq, cap, heads), out_shap...]
where the time goes in v3:
time: 87.1 us; the launch traced here: 85.8 us
  Pallas kernels  85.2 us (98%)
    pallas_call x1, Pallas kernels, local(): pl.pallas_call(functools.partial(main_kernel, nseq, cap, heads), out_shap...  81.1 us
    pallas_call x1, Pallas kernels, local(): pl.pallas_call(functools.partial(last_kernel, nseq, cap), out_shape=(jax....  4.1 us

profile of v3, /device:TPU:32, one launch (start us, length us, event | category | flops | bytes accessed | tf_op | source)
XLA Modules:
  0.0 85.8 jit_solution(105595671276632957)
XLA Ops:
  0.6 81.1 %shard_map.86 = (bf16[8,64,512]{2,1,0:T(8,128)(2,1)}, bf16[64,512]{1,0:T(8,128)(2,1)}, bf16[16,2,112,128]{3,2,1,0:T(8,128)(2,1)}, s32[16,1,128]{2,1,0:T(1,128)}) custom-call(s32[2,8]{1,0:T(2,128)} %bitcast.6, s32[2,8]{1,0:T(2,128)} %bitcast.7, bf16[512,512]{1,0:T(8,128)(2,1)} %q_h.1, bf16[512,512]{1,0:T(8,128)(2,1)} %g_h.1, bf16[64,112,128]{2,1,0:T(8,128)(2,1)} %tab_h.1, ...), custom_call_target="tpu_custom_call" | custom-call | tf_op jit(solution)/shard_map/pallas_call | solution.py:419
  81.7 4.1 %shard_map.87 = (bf16[512,512]{1,0:T(8,128)(2,1)}, f32[64,112,128]{2,1,0:T(8,128)}) custom-call(s32[16,1,128]{2,1,0:T(1,128)} %get-tuple-element.6.reqs_h, bf16[16,2,112,128]{3,2,1,0:T(8,128)(2,1)} %get-tuple-element.7.back_h, bf16[8,64,512]{2,1,0:T(8,128)(2,1)} %get-tuple-element.8.dq_h, bf16[64,512]{1,0:T(8,128)(2,1)} %get-tuple-element.9.prev_h), custom_call_target="tpu_custom_call" | custom-call | tf_op jit(solution)/shard_map/pallas_call | solution.py:479

commit v4 on v3

--- a/solution.py
+++ b/solution.py
@@ -55,6 +55,10 @@
     following = (base + (s + 1) % ring, e)
     preceding = (base + (s + ring - 1) % ring, e)
 
+    def peer_of(i):
+        i = 1 + (i + nseq // 2) % (nseq - 1)
+        return ((s // ring + i // ring) % (nseq // ring)) * ring + (s % ring + i % ring) % ring
+
     def remote(src, dst, sem, where):
         return pltpu.make_async_remote_copy(
             src_ref=src, dst_ref=dst, send_sem=sem.at[0], recv_sem=sem.at[1],
@@ -64,7 +68,7 @@
     barrier = pltpu.get_barrier_semaphore()
 
     def greet(i, _):
-        pl.semaphore_signal(barrier, inc=1, device_id=((s + i) % nseq, e), device_id_type=MESH)
+        pl.semaphore_signal(barrier, inc=1, device_id=(peer_of(i), e), device_id_type=MESH)
         return 0
 
     lax.fori_loop(1, nseq, greet, 0)
@@ -117,7 +121,7 @@
     pl.semaphore_wait(barrier, nseq - 1 + 3)
 
     def id_copy(i):
-        return remote(req, reqs.at[s], id_sem.at[i], ((s + i) % nseq, e))
+        return remote(req, reqs.at[s], id_sem.at[i], (peer_of(i), e))
 
     def send_ids(i, _):
         id_copy(i).start()
@@ -164,11 +168,11 @@
     reqs_copy.wait()
 
     def a_copy(i):
-        peer = (s + i) % nseq
+        peer = peer_of(i)
         return remote(send_a.at[peer], recv_a.at[s], a_sem.at[i], (peer, e))
 
     def send_rows(i, _):
-        peer = (s + i) % nseq
+        peer = peer_of(i)
         for k in range(cap):
             wanted = jnp.maximum(reqs_s[peer, 0, s * cap + k], 0)
             send_a[peer, k] = tab[wanted]
@@ -325,11 +329,11 @@
     dq_out.start()
 
     def e_copy(i):
-        peer = (s + i) % nseq
+        peer = peer_of(i)
         return remote(send_b.at[peer], back_o.at[s], e_sem.at[i], (peer, e))
 
     def send_terms(i, _):
-        peer = (s + i) % nseq
+        peer = peer_of(i)
         for k in range(cap):
             send_b[peer, k] = res[uos_s[0, peer * cap + k]]
         e_copy(i).start()
@@ -381,26 +385,28 @@
     s = lax.axis_index("seq")
     rows = dquery_o.shape[0]
     per_seq = SEQ_LEN // rows
-    for c in ins:
-        c.wait()
-
-    def add(i, _):
-        row = reqs_s[i // cap, 0, s * cap + i % cap]
-
-        @pl.when(row >= 0)
-        def _():
-            total[row] += back[i // cap, i % cap].astype(F32)
-
-        return 0
-
-    lax.fori_loop(0, nseq * cap, add, 0)
-    table_out = pltpu.make_async_copy(total, dtable_o, sem.at[4])
-    table_out.start()
+    ins[1].wait()
+    ins[2].wait()
     shift[pl.ds(0, M), :] = prev[...].astype(F32) * (s % per_seq != 0).astype(F32)
     shift[pl.ds(M, rows), :] = dq[...].reshape(rows, dq.shape[2]).astype(F32)
     moved[...] = shift[pl.ds(1, rows), :].astype(BF16)
     query_out = pltpu.make_async_copy(moved, dquery_o, sem.at[5])
     query_out.start()
+    ins[0].wait()
+    ins[3].wait()
+
+    def add(i, _):
+        row = reqs_s[i // cap, 0, s * cap + i % cap]
+
+        @pl.when(row >= 0)
+        def _():
+            total[row] += back[i // cap, i % cap].astype(F32)
+
+        return 0
+
+    lax.fori_loop(0, nseq * cap, add, 0)
+    table_out = pltpu.make_async_copy(total, dtable_o, sem.at[4])
+    table_out.start()
     table_out.wait()
     query_out.wait()
 

time: 87.1 us -> 85.5 us (0.982); the launches traced: 85.8 us -> 85.3 us
  no operation moved by 1% of the time
where the time goes in v4:
time: 85.5 us; the launch traced here: 85.3 us
  Pallas kernels  84.6 us (99%)
    pallas_call x1, Pallas kernels, local(): pl.pallas_call(functools.partial(main_kernel, nseq, cap, heads), out_shap...  80.7 us
    pallas_call x1, Pallas kernels, local(): pl.pallas_call(functools.partial(last_kernel, nseq, cap), out_shape=(jax....  3.92 us

profile of v4, /device:TPU:32, one launch (start us, length us, event | category | flops | bytes accessed | tf_op | source)
XLA Modules:
  0.0 85.3 jit_solution(537783983501699270)
XLA Ops:
  0.6 80.7 %shard_map.86 = (bf16[8,64,512]{2,1,0:T(8,128)(2,1)}, bf16[64,512]{1,0:T(8,128)(2,1)}, bf16[16,2,112,128]{3,2,1,0:T(8,128)(2,1)}, s32[16,1,128]{2,1,0:T(1,128)}) custom-call(s32[2,8]{1,0:T(2,128)} %bitcast.6, s32[2,8]{1,0:T(2,128)} %bitcast.7, bf16[512,512]{1,0:T(8,128)(2,1)} %q_h.1, bf16[512,512]{1,0:T(8,128)(2,1)} %g_h.1, bf16[64,112,128]{2,1,0:T(8,128)(2,1)} %tab_h.1, ...), custom_call_target="tpu_custom_call" | custom-call | tf_op jit(solution)/shard_map/pallas_call | solution.py:425
  81.4 3.9 %shard_map.87 = (bf16[512,512]{1,0:T(8,128)(2,1)}, f32[64,112,128]{2,1,0:T(8,128)}) custom-call(s32[16,1,128]{2,1,0:T(1,128)} %get-tuple-element.6.reqs_h, bf16[16,2,112,128]{3,2,1,0:T(8,128)(2,1)} %get-tuple-element.7.back_h, bf16[8,64,512]{2,1,0:T(8,128)(2,1)} %get-tuple-element.8.dq_h, bf16[64,512]{1,0:T(8,128)(2,1)} %get-tuple-element.9.prev_h), custom_call_target="tpu_custom_call" | custom-call | tf_op jit(solution)/shard_map/pallas_call | solution.py:485
